TPU v7x, 256 devices: a whole 4x4x8 slice. The times are simulated.
256 devices in a mesh: row: 16 (over y, x), col: 16 (over z, core).
Axes of the slice: x: 4, y: 4, z: 8, core: 2. Of those that a mesh axis runs over, the one named last changes fastest.
Arguments:
- matrix: bfloat16 [24576, 24576], P('row', 'col'), may hold values from -6 to 6
- inverses: bfloat16 [2, 256, 256], replicated, may hold values from -0.09 to 0.1, as said below
Outputs:
- factored: bfloat16 [24576, 24576], P('row', 'col')
- panels: bfloat16 [24576, 512], P('row')
Inputs may be any that keep to these rules, and one draw needn't show every extreme that they name: `inverses`: each of the two matrices is lower triangular with a diagonal between 0.05 and 0.1.
All inputs are finite; a program needn't handle non-finite values.
Results may differ from a plain program's by a relative error of at most 0.0057.
Values may be sent and summed in bfloat16 or wider, within the bound.
No kernel may reach another device: no remote copies, remote signals or barrier semaphores. Data moves between devices by JAX's collectives and lax.ppermute only.
A program may use at most 128 MiB of HBM per device.

v0:
```python
import jax
import jax.numpy as jnp
from jax import lax
from jax.sharding import PartitionSpec as P


def from_root(value, axis, source):
    kept = jnp.where(lax.axis_index(axis) == source, value, 0).astype(value.dtype)
    return lax.psum(kept, axis)


def outer_term(left_rows, right_rows):
    return lax.dot_general(
        left_rows, right_rows, (((1,), (1,)), ((), ())), preferred_element_type=jnp.float32
    )


def shards(matrix, inverses):
    width = inverses.shape[1]
    rows_local = matrix.shape[0]
    row_count = lax.axis_size("row")
    col_count = lax.axis_size("col")
    row_rank = lax.axis_index("row")
    col_rank = lax.axis_index("col")
    blocks_row = rows_local // width
    blocks_col = matrix.shape[1] // width
    ratio_blocks = col_count // row_count
    global_rows = jnp.repeat(jnp.arange(blocks_row, dtype=jnp.int32) * row_count + row_rank, width)
    source_row = col_rank % row_count
    source_slot = col_rank // row_count

    def factor(panel, inverse, start_block, owner_col):
        product = jnp.dot(panel, inverse.T, preferred_element_type=jnp.float32)
        masked = jnp.where((global_rows >= start_block)[:, None], product, 0.0).astype(jnp.bfloat16)
        return from_root(masked, "col", owner_col)

    def columns_of(left_rows):
        gathered = lax.all_gather(left_rows, "row", axis=0, tiled=True)
        gathered = gathered.reshape(row_count, blocks_col, ratio_blocks, width, width)
        mine = lax.dynamic_index_in_dim(gathered, source_row, 0, keepdims=False)
        mine = lax.dynamic_index_in_dim(mine, source_slot, 1, keepdims=False)
        return mine.reshape(blocks_col * width, width)

    first_rows = factor(matrix[:, :width], inverses[0], 1, 0)
    first_cols = columns_of(first_rows)
    partial_value = matrix.astype(jnp.float32) - outer_term(first_rows, first_cols)
    head = partial_value[:, :width].astype(jnp.bfloat16)
    second_rows = factor(head, inverses[1], 2, 1)
    second_cols = columns_of(second_rows)
    factored = (partial_value - outer_term(second_rows, second_cols)).astype(jnp.bfloat16)
    return (factored, jnp.concatenate([first_rows, second_rows], axis=1))


def solution(mesh):
    return jax.shard_map(
        shards,
        mesh=mesh,
        in_specs=(P("row", "col"), P()),
        out_specs=(P("row", "col"), P("row", None)),
        check_vma=False,
    )
```

profile of v0, /device:TPU:1, one launch (start us, length us, event | category | flops | bytes accessed | tf_op | source)
XLA Modules:
  0.0 456.7 jit_solution(4977230878266750554)
XLA Ops:
  7.2 0.0 all-reduce.3.cloned.1.call-start
  7.2 0.1 broadcast_in_dim.30
  7.3 2.5 fusion.4
  9.8 0.0 all-reduce.3.cloned.1.call-update
  9.8 0.0 all-gather.3.cloned.1.call-start
  9.9 115.4 %all-reduce.3.cloned.1.call-done = bf16[1536,256]{1,0:T(8,128)(2,1)} async-done(((bf16[1536,256]{1,0:T(8,128)(2,1)}), bf16[1536,256]{1,0:T(8,128)(2,1)}) %all-reduce.3.cloned.1.call-update) | async-done | bytes 786448 | tf_op jit(solution)/shard_map/psum | solution.py:9
  125.2 0.0 all-gather.3.cloned.1.call-update
  125.3 0.0 all-reduce.5.cloned.1.call-start
  125.3 0.1 broadcast_in_dim.34
  125.4 98.0 %all-gather.3.cloned.1.call-done = bf16[24576,256]{1,0:T(8,128)(2,1)} async-done(((bf16[1536,256]{1,0:T(8,128)(2,1)}), bf16[24576,256]{1,0:T(8,128)(2,1)}) %all-gather.3.cloned.1.call-update) | async-done | bytes 12582928 | tf_op jit(solution)/shard_map/all_gather | solution.py:38
  223.4 1.2 constant_dynamic-slice_fusion.1
  224.6 0.0 copy-start.3
  224.6 4.0 convolution_subtract_fusion.1
  228.6 0.0 copy-start
  228.7 3.5 copy-done
  232.2 0.0 copy-done.3
  232.2 0.0 copy-start.1
  232.2 1.3 fusion.3
  233.5 0.0 all-reduce.5.cloned.1.call-update
  233.5 0.0 all-gather.5.cloned.1.call-start
  233.6 110.4 %all-reduce.5.cloned.1.call-done = bf16[1536,256]{1,0:T(8,128)(2,1)} async-done(((bf16[1536,256]{1,0:T(8,128)(2,1)}), bf16[1536,256]{1,0:T(8,128)(2,1)}) %all-reduce.5.cloned.1.call-update) | async-done | bytes 786448 | tf_op jit(solution)/shard_map/psum | solution.py:9
  343.9 0.0 copy-start.2
  343.9 0.0 all-gather.5.cloned.1.call-update
  343.9 0.0 copy-done.1
  344.0 2.5 pad_maximum_fusion
  346.4 95.2 %all-gather.5.cloned.1.call-done = bf16[24576,256]{1,0:T(8,128)(2,1)} async-done(((bf16[1536,256]{1,0:T(8,128)(2,1)}), bf16[24576,256]{1,0:T(8,128)(2,1)}) %all-gather.5.cloned.1.call-update) | async-done | bytes 12582928 | tf_op jit(solution)/shard_map/all_gather | solution.py:38
  441.6 1.2 constant_dynamic-slice_fusion
  442.8 0.0 copy-done.2
  442.8 7.3 %fusion = bf16[1536,1536]{1,0:T(8,128)(2,1)} fusion(f32[1536,1536]{1,0:T(8,128)} %copy-done, bf16[1536,256]{1,0:T(8,128)(2,1)S(1)} %copy-done.2, bf16[1536,256]{1,0:T(8,128)(2,1)S(1)} %bitcast.15), kind=kOutput, calls=%fused_computation.2 | convolution fusion | flops 1212678144 | bytes 15728640 | tf_op jit(solution)/shard_map/dot_general | solution.py:13
  (3 shorter events, 0.0 us)
Async XLA Ops:
  7.2 118.1 %all-reduce.3.cloned.1.call-start = ((), (), s32[]{:S(2)}) async-start(), calls=%async_computation | async-start | bytes 1572864 | tf_op jit(solution)/shard_map/psum | solution.py:9
  9.8 213.6 %all-gather.3.cloned.1.call-start = ((), (), s32[]{:S(2)}) async-start(), calls=%async_computation.1 | async-start | bytes 13369344 | tf_op jit(solution)/shard_map/all_gather | solution.py:38
  125.3 218.7 %all-reduce.5.cloned.1.call-start = ((), (), s32[]{:S(2)}) async-start(), calls=%async_computation.2 | async-start | bytes 1572864 | tf_op jit(solution)/shard_map/psum | solution.py:9
  224.6 7.6 %copy-start.3 = (bf16[2,256,256]{2,1,0:T(8,128)(2,1)S(1)}, bf16[2,256,256]{2,1,0:T(8,128)(2,1)}, u32[]{:S(2)}) copy-start(bf16[2,256,256]{2,1,0:T(8,128)(2,1)} %param.3) | copy-start | bytes 786436
  228.6 3.5 copy-start
  232.2 111.8 %copy-start.1 = (bf16[1536,256]{1,0:T(8,128)(2,1)S(1)}, bf16[1536,256]{1,0:T(8,128)(2,1)}, u32[]{:S(2)}) copy-start(bf16[1536,256]{1,0:T(8,128)(2,1)} %all-reduce.3.cloned.1.call-done) | copy-start | bytes 2359300
  233.5 208.1 %all-gather.5.cloned.1.call-start = ((), (), s32[]{:S(2)}) async-start(), calls=%async_computation.3 | async-start | bytes 13369344 | tf_op jit(solution)/shard_map/all_gather | solution.py:38
  343.9 98.9 %copy-start.2 = (bf16[1536,256]{1,0:T(8,128)(2,1)S(1)}, bf16[1536,256]{1,0:T(8,128)(2,1)}, u32[]{:S(2)}) copy-start(bf16[1536,256]{1,0:T(8,128)(2,1)} %all-reduce.5.cloned.1.call-done) | copy-start | bytes 2359300
Sparse Core Ops, SparseCore 0:
  10.9 114.2 all-reduce.2
  128.0 95.3 all-gather.2
  233.6 110.2 all-reduce.4
  346.2 95.3 all-gather.4
where the time goes:
time: 457 us
  waiting for transfers between devices  419 us (92%)
  matrix products  15.1 us (3%)
  between operations  13.8 us (3%)
  local copies, waits for them, and re-layouts  6.09 us (1%)
    psum x2, waiting for transfers between devices, from_root(): return lax.psum(kept, axis)  226 us
    all_gather x2, waiting for transfers between devices, columns_of(): gathered = lax.all_gather(left_rows, 'row', axis=0, tiled=True)  193 us
    dot_general x2, matrix products, outer_term(): lax.dot_general(left_rows, right_rows, (((1,), (1,)), ((), ())), preferre...  11.3 us
  transfers between devices with their start and end apart: 4, of which 4 were waited for; matrix products, arithmetic and copies ran while one was open for 1% of the time, Pallas kernels for 0%

commit v1 on v0

--- a/solution.py
+++ b/solution.py
@@ -6,7 +6,7 @@
 
 def from_root(value, axis, source):
     kept = jnp.where(lax.axis_index(axis) == source, value, 0).astype(value.dtype)
-    return lax.psum(kept, axis)
+    return lax.all_gather(kept, axis_name=axis).sum(axis=0)
 
 
 def outer_term(left_rows, right_rows):

time: 457 us -> 393 us (0.86)
  waiting for transfers between devices: 419 us -> 340 us
  other arithmetic: 2.46 us -> 17.4 us
    psum x2 -> x0, waiting for transfers between devices: 226 us -> none  [from_root(): return lax.psum(kept, axis)]
    all_gather x0 -> x2, waiting for transfers between devices: none -> 156 us  [from_root(): return lax.all_gather(kept, axis_name=axis).sum(axis=0)]
    reduce_sum x0 -> x2, other arithmetic: none -> 14.9 us  [from_root(): return lax.all_gather(kept, axis_name=axis).sum(axis=0)]
    all_gather x2, waiting for transfers between devices: 193 us -> 184 us  [columns_of(): gathered = lax.all_gather(left_rows, 'row', axis=0, tiled=True)]
where the time goes in v1:
time: 393 us
  waiting for transfers between devices  340 us (87%)
  other arithmetic  17.4 us (4%)
  matrix products  15.1 us (4%)
  between operations  13.8 us (4%)
  local copies, waits for them, and re-layouts  6.09 us (2%)
    all_gather x2, waiting for transfers between devices, columns_of(): gathered = lax.all_gather(left_rows, 'row', axis=0, tiled=True)  184 us
    all_gather x2, waiting for transfers between devices, from_root(): return lax.all_gather(kept, axis_name=axis).sum(axis=0)  156 us
    reduce_sum x2, other arithmetic, from_root(): return lax.all_gather(kept, axis_name=axis).sum(axis=0)  14.9 us
    dot_general x2, matrix products, outer_term(): lax.dot_general(left_rows, right_rows, (((1,), (1,)), ((), ())), preferre...  11.3 us
  transfers between devices with their start and end apart: 4, of which 4 were waited for; matrix products, arithmetic and copies ran while one was open for 1% of the time, Pallas kernels for 0%

profile of v1, /device:TPU:1, one launch (start us, length us, event | category | flops | bytes accessed | tf_op | source)
XLA Modules:
  0.0 393.0 jit_solution(13717554364815691284)
XLA Ops:
  7.2 0.0 all-gather.11.cloned.1.call-start
  7.2 0.1 broadcast_in_dim.30
  7.3 2.5 fusion.4
  9.8 0.0 all-gather.11.cloned.1.call-update
  9.8 0.0 all-gather.7.cloned.1.call-start
  9.9 80.5 %all-gather.11.cloned.1.call-done = bf16[24576,256]{1,0:T(8,128)(2,1)} async-done(((bf16[1536,256]{1,0:T(8,128)(2,1)}), bf16[24576,256]{1,0:T(8,128)(2,1)}) %all-gather.11.cloned.1.call-update) | async-done | bytes 12582928 | tf_op jit(solution)/shard_map/all_gather | solution.py:9
  90.3 7.4 %reduce_sum.24 = bf16[1536,256]{1,0:T(8,128)(2,1)} reduce(bf16[16,1536,256]{2,1,0:T(8,128)(2,1)} %bitcast.17, bf16[]{:T(256)} %constant.50.clone.1), dimensions={0}, to_apply=%region_0.1 | reduce | flops 5898240 | bytes 13369346 | tf_op jit(solution)/shard_map/reduce_sum | solution.py:9
  97.8 0.0 all-gather.7.cloned.1.call-update
  97.8 0.0 all-gather.13.cloned.1.call-start
  97.8 0.1 broadcast_in_dim.34
  97.9 93.1 %all-gather.7.cloned.1.call-done = bf16[24576,256]{1,0:T(8,128)(2,1)} async-done(((bf16[1536,256]{1,0:T(8,128)(2,1)}), bf16[24576,256]{1,0:T(8,128)(2,1)}) %all-gather.7.cloned.1.call-update) | async-done | bytes 12582928 | tf_op jit(solution)/shard_map/all_gather | solution.py:38
  191.1 1.2 constant_dynamic-slice_fusion.1
  192.3 0.0 copy-start.3
  192.3 4.0 %convolution_subtract_fusion.1 = f32[1536,1536]{1,0:T(8,128)S(1)} fusion(bf16[1536,256]{1,0:T(8,128)(2,1)} %reduce_sum.24, bf16[1536,256]{1,0:T(8,128)(2,1)S(1)} %bitcast.18, bf16[1536,1536]{1,0:T(8,128)(2,1)} %param.2), kind=kOutput, calls=%fused_computation.1 | convolution fusion | flops 1212678144 | bytes 15728640 | tf_op jit(solution)/shard_map/dot_general | solution.py:13
  196.3 0.0 copy-start
  196.3 3.5 copy-done
  199.9 0.0 copy-done.3
  199.9 1.3 fusion.3
  201.2 0.0 all-gather.13.cloned.1.call-update
  201.2 0.0 all-gather.9.cloned.1.call-start
  201.2 75.9 %all-gather.13.cloned.1.call-done = bf16[24576,256]{1,0:T(8,128)(2,1)} async-done(((bf16[1536,256]{1,0:T(8,128)(2,1)}), bf16[24576,256]{1,0:T(8,128)(2,1)}) %all-gather.13.cloned.1.call-update) | async-done | bytes 12582928 | tf_op jit(solution)/shard_map/all_gather | solution.py:9
  277.2 0.0 copy-start.1
  277.2 7.5 %reduce_sum.25 = bf16[1536,256]{1,0:T(8,128)(2,1)} reduce(bf16[16,1536,256]{2,1,0:T(8,128)(2,1)} %bitcast.16, bf16[]{:T(256)} %constant.50.clone.1), dimensions={0}, to_apply=%region_1.2 | reduce | flops 5898240 | bytes 13369346 | tf_op jit(solution)/shard_map/reduce_sum | solution.py:9
  284.7 0.0 copy-start.2
  284.7 0.0 all-gather.9.cloned.1.call-update
  284.7 0.0 copy-done.1
  284.7 2.5 pad_maximum_fusion
  287.2 90.8 %all-gather.9.cloned.1.call-done = bf16[24576,256]{1,0:T(8,128)(2,1)} async-done(((bf16[1536,256]{1,0:T(8,128)(2,1)}), bf16[24576,256]{1,0:T(8,128)(2,1)}) %all-gather.9.cloned.1.call-update) | async-done | bytes 12582928 | tf_op jit(solution)/shard_map/all_gather | solution.py:38
  378.0 1.2 constant_dynamic-slice_fusion
  379.2 0.0 copy-done.2
  379.2 7.3 %fusion = bf16[1536,1536]{1,0:T(8,128)(2,1)} fusion(f32[1536,1536]{1,0:T(8,128)} %copy-done, bf16[1536,256]{1,0:T(8,128)(2,1)S(1)} %copy-done.2, bf16[1536,256]{1,0:T(8,128)(2,1)S(1)} %bitcast.19), kind=kOutput, calls=%fused_computation.2 | convolution fusion | flops 1212678144 | bytes 15728640 | tf_op jit(solution)/shard_map/dot_general | solution.py:13
  (3 shorter events, 0.0 us)
Async XLA Ops:
  7.2 83.2 %all-gather.11.cloned.1.call-start = ((), (), s32[]{:S(2)}) async-start(), calls=%async_computation.2 | async-start | bytes 13369344 | tf_op jit(solution)/shard_map/all_gather | solution.py:9
  9.8 181.3 %all-gather.7.cloned.1.call-start = ((), (), s32[]{:S(2)}) async-start(), calls=%async_computation | async-start | bytes 13369344 | tf_op jit(solution)/shard_map/all_gather | solution.py:38
  97.8 179.4 %all-gather.13.cloned.1.call-start = ((), (), s32[]{:S(2)}) async-start(), calls=%async_computation.3 | async-start | bytes 13369344 | tf_op jit(solution)/shard_map/all_gather | solution.py:9
  192.3 7.6 %copy-start.3 = (bf16[2,256,256]{2,1,0:T(8,128)(2,1)S(1)}, bf16[2,256,256]{2,1,0:T(8,128)(2,1)}, u32[]{:S(2)}) copy-start(bf16[2,256,256]{2,1,0:T(8,128)(2,1)} %param.3) | copy-start | bytes 786436
  196.3 3.5 copy-start
  201.2 176.8 %all-gather.9.cloned.1.call-start = ((), (), s32[]{:S(2)}) async-start(), calls=%async_computation.1 | async-start | bytes 13369344 | tf_op jit(solution)/shard_map/all_gather | solution.py:38
  277.2 7.5 %copy-start.1 = (bf16[1536,256]{1,0:T(8,128)(2,1)S(1)}, bf16[1536,256]{1,0:T(8,128)(2,1)}, u32[]{:S(2)}) copy-start(bf16[1536,256]{1,0:T(8,128)(2,1)} %reduce_sum.24) | copy-start | bytes 2359300
  284.7 94.5 %copy-start.2 = (bf16[1536,256]{1,0:T(8,128)(2,1)S(1)}, bf16[1536,256]{1,0:T(8,128)(2,1)}, u32[]{:S(2)}) copy-start(bf16[1536,256]{1,0:T(8,128)(2,1)} %reduce_sum.25) | copy-start | bytes 2359300
Sparse Core Ops, SparseCore 0:
  10.4 79.8 all-gather.10
  97.9 93.1 all-gather.6
  201.3 75.8 all-gather.12
  284.8 93.1 all-gather.8

commit v2 on v0

--- a/solution.py
+++ b/solution.py
@@ -2,6 +2,11 @@
 import jax.numpy as jnp
 from jax import lax
 from jax.sharding import PartitionSpec as P
+
+
+def all_by_exchange(value, name, along):
+    stack = jnp.stack([value] * lax.axis_size(name))
+    return jnp.concatenate(lax.all_to_all(stack, name, 0, 0), axis=along)
 
 
 def from_root(value, axis, source):
@@ -35,7 +40,7 @@
         return from_root(masked, "col", owner_col)
 
     def columns_of(left_rows):
-        gathered = lax.all_gather(left_rows, "row", axis=0, tiled=True)
+        gathered = all_by_exchange(left_rows, "row", 0)
         gathered = gathered.reshape(row_count, blocks_col, ratio_blocks, width, width)
         mine = lax.dynamic_index_in_dim(gathered, source_row, 0, keepdims=False)
         mine = lax.dynamic_index_in_dim(mine, source_slot, 1, keepdims=False)

time: 457 us -> 665 us (1.46)
  waiting for transfers between devices: 419 us -> 596 us
  local copies, waits for them, and re-layouts: 6.09 us -> 19.8 us
  starting transfers between devices: 0.16 us -> 13.5 us
    all_to_all x0 -> x2, waiting for transfers between devices: none -> 369 us  [all_by_exchange(): return jnp.concatenate(lax.all_to_all(stack, name, 0, 0), axis=along)]
    all_gather x2 -> x0, waiting for transfers between devices: 193 us -> none  [columns_of(): gathered = lax.all_gather(left_rows, 'row', axis=0, tiled=True)]
    another operation x0 -> x2, local copies, waits for them, and re-layouts: none -> 13.6 us  [all_by_exchange(): stack = jnp.stack([value] * lax.axis_size(name))]
    all_to_all x0 -> x2, starting transfers between devices: none -> 13.4 us  [all_by_exchange(): return jnp.concatenate(lax.all_to_all(stack, name, 0, 0), axis=along)]
  transfers between devices with their start and end apart: 4 -> 4, of which waited for: 4 -> 4; matrix products, arithmetic and copies ran while one was open for 1% -> 0% of each run, Pallas kernels for 0% -> 0%
where the time goes in v2:
time: 665 us; the launch traced here: 660 us
  waiting for transfers between devices  596 us (90%)
  local copies, waits for them, and re-layouts  19.8 us (3%)
  matrix products  14.9 us (2%)
  between operations  14.1 us (2%)
  starting transfers between devices  13.5 us (2%)
    all_to_all x2, waiting for transfers between devices, all_by_exchange(): return jnp.concatenate(lax.all_to_all(stack, name, 0, 0), axis=along)  369 us
    psum x2, waiting for transfers between devices, from_root(): return lax.psum(kept, axis)  227 us
    another operation x2, local copies, waits for them, and re-layouts, all_by_exchange(): stack = jnp.stack([value] * lax.axis_size(name))  13.6 us
    all_to_all x2, starting transfers between devices, all_by_exchange(): return jnp.concatenate(lax.all_to_all(stack, name, 0, 0), axis=along)  13.4 us
  transfers between devices with their start and end apart: 4, of which 4 were waited for; matrix products, arithmetic and copies ran while one was open for 0% of the time, Pallas kernels for 0%

profile of v2, /device:TPU:1, one launch (start us, length us, event | category | flops | bytes accessed | tf_op | source)
XLA Modules:
  0.0 659.8 jit_solution(13167815841436633145)
XLA Ops:
  7.2 0.0 all-reduce.3.cloned.1.call-start
  7.2 0.1 broadcast_in_dim.30
  7.3 2.5 fusion.4
  9.8 0.0 all-reduce.3.cloned.1.call-update
  9.8 115.4 %all-reduce.3.cloned.1.call-done = bf16[1536,256]{1,0:T(8,128)(2,1)} async-done(((bf16[1536,256]{1,0:T(8,128)(2,1)}), bf16[1536,256]{1,0:T(8,128)(2,1)}) %all-reduce.3.cloned.1.call-update) | async-done | bytes 786448 | tf_op jit(solution)/shard_map/psum | solution.py:14
  125.2 6.8 %stack.4 = bf16[16,1536,256]{2,1,0:T(8,128)(2,1)} broadcast(bf16[1536,256]{1,0:T(8,128)(2,1)} %all-reduce.3.cloned.1.call-done), dimensions={1,2} | broadcast | bytes 13369344 | tf_op jit(solution)/shard_map/stack | solution.py:8
  132.1 0.0 copy-start.1
  132.1 6.7 %all-to-all-start = ((bf16[16,1536,256]{2,1,0:T(8,128)(2,1)}), bf16[16,1536,256]{2,1,0:T(8,128)(2,1)}, u32[]{:S(2)}, u32[]{:S(2)}) async-start(bf16[16,1536,256]{2,1,0:T(8,128)(2,1)} %stack.4), calls=%async_computation | async-start | bytes 25165824 | tf_op jit(solution)/shard_map/all_to_all | solution.py:9
  138.8 0.0 all-reduce.5.cloned.1.call-start
  138.8 0.1 broadcast_in_dim.34
  138.9 185.2 %all-to-all-done = bf16[16,1536,256]{2,1,0:T(8,128)(2,1)} async-done(((bf16[16,1536,256]{2,1,0:T(8,128)(2,1)}), bf16[16,1536,256]{2,1,0:T(8,128)(2,1)}, u32[]{:S(2)}, u32[]{:S(2)}) %all-to-all-start) | async-done | bytes 12582944 | tf_op jit(solution)/shard_map/all_to_all | solution.py:9
  324.1 1.2 constant_dynamic-slice_fusion.1
  325.3 0.0 copy-done.1
  325.3 0.0 copy-start.3
  325.3 3.8 convolution_subtract_fusion.1
  329.1 0.0 copy-start
  329.1 3.6 copy-done
  332.7 0.0 copy-done.3
  332.7 1.3 fusion.3
  334.0 0.0 all-reduce.5.cloned.1.call-update
  334.0 111.6 %all-reduce.5.cloned.1.call-done = bf16[1536,256]{1,0:T(8,128)(2,1)} async-done(((bf16[1536,256]{1,0:T(8,128)(2,1)}), bf16[1536,256]{1,0:T(8,128)(2,1)}) %all-reduce.5.cloned.1.call-update) | async-done | bytes 786448 | tf_op jit(solution)/shard_map/psum | solution.py:14
  445.6 6.8 %stack.5 = bf16[16,1536,256]{2,1,0:T(8,128)(2,1)} broadcast(bf16[1536,256]{1,0:T(8,128)(2,1)} %all-reduce.5.cloned.1.call-done), dimensions={1,2} | broadcast | bytes 13369344 | tf_op jit(solution)/shard_map/stack | solution.py:8
  452.4 0.0 copy-start.2
  452.4 6.7 %all-to-all-start.1 = ((bf16[16,1536,256]{2,1,0:T(8,128)(2,1)}), bf16[16,1536,256]{2,1,0:T(8,128)(2,1)}, u32[]{:S(2)}, u32[]{:S(2)}) async-start(bf16[16,1536,256]{2,1,0:T(8,128)(2,1)} %stack.5), calls=%async_computation.1 | async-start | bytes 25165824 | tf_op jit(solution)/shard_map/all_to_all | solution.py:9
  459.1 0.0 copy-done.2
  459.1 1.3 pad_maximum_fusion
  460.4 184.0 %all-to-all-done.1 = bf16[16,1536,256]{2,1,0:T(8,128)(2,1)} async-done(((bf16[16,1536,256]{2,1,0:T(8,128)(2,1)}), bf16[16,1536,256]{2,1,0:T(8,128)(2,1)}, u32[]{:S(2)}, u32[]{:S(2)}) %all-to-all-start.1) | async-done | bytes 12582944 | tf_op jit(solution)/shard_map/all_to_all | solution.py:9
  644.4 1.2 constant_dynamic-slice_fusion
  645.6 7.3 %fusion = bf16[1536,1536]{1,0:T(8,128)(2,1)} fusion(f32[1536,1536]{1,0:T(8,128)} %copy-done, bf16[1536,256]{1,0:T(8,128)(2,1)S(1)} %copy-done.2, bf16[1536,256]{1,0:T(8,128)(2,1)S(1)} %bitcast.15), kind=kOutput, calls=%fused_computation.2 | convolution fusion | flops 1212678144 | bytes 15728640 | tf_op jit(solution)/shard_map/dot_general | solution.py:18
  (3 shorter events, 0.0 us)
Async XLA Ops:
  7.2 118.1 %all-reduce.3.cloned.1.call-start = ((), (), s32[]{:S(2)}) async-start(), calls=%async_computation.2 | async-start | bytes 1572864 | tf_op jit(solution)/shard_map/psum | solution.py:14
  132.1 193.2 %copy-start.1 = (bf16[1536,256]{1,0:T(8,128)(2,1)S(1)}, bf16[1536,256]{1,0:T(8,128)(2,1)}, u32[]{:S(2)}) copy-start(bf16[1536,256]{1,0:T(8,128)(2,1)} %all-reduce.3.cloned.1.call-done) | copy-start | bytes 2359300
  132.1 192.0 %all-to-all-start = ((bf16[16,1536,256]{2,1,0:T(8,128)(2,1)}), bf16[16,1536,256]{2,1,0:T(8,128)(2,1)}, u32[]{:S(2)}, u32[]{:S(2)}) async-start(bf16[16,1536,256]{2,1,0:T(8,128)(2,1)} %stack.4), calls=%async_computation | async-start | bytes 25165824 | tf_op jit(solution)/shard_map/all_to_all | solution.py:9
  138.8 306.8 %all-reduce.5.cloned.1.call-start = ((), (), s32[]{:S(2)}) async-start(), calls=%async_computation.3 | async-start | bytes 1572864 | tf_op jit(solution)/shard_map/psum | solution.py:14
  325.3 7.4 %copy-start.3 = (bf16[2,256,256]{2,1,0:T(8,128)(2,1)S(1)}, bf16[2,256,256]{2,1,0:T(8,128)(2,1)}, u32[]{:S(2)}) copy-start(bf16[2,256,256]{2,1,0:T(8,128)(2,1)} %param.3) | copy-start | bytes 786436
  329.1 3.6 copy-start
  452.4 6.7 %copy-start.2 = (bf16[1536,256]{1,0:T(8,128)(2,1)S(1)}, bf16[1536,256]{1,0:T(8,128)(2,1)}, u32[]{:S(2)}) copy-start(bf16[1536,256]{1,0:T(8,128)(2,1)} %all-reduce.5.cloned.1.call-done) | copy-start | bytes 2359300
  452.4 192.0 %all-to-all-start.1 = ((bf16[16,1536,256]{2,1,0:T(8,128)(2,1)}), bf16[16,1536,256]{2,1,0:T(8,128)(2,1)}, u32[]{:S(2)}, u32[]{:S(2)}) async-start(bf16[16,1536,256]{2,1,0:T(8,128)(2,1)} %stack.5), calls=%async_computation.1 | async-start | bytes 25165824 | tf_op jit(solution)/shard_map/all_to_all | solution.py:9
Sparse Core Ops, SparseCore 0:
  10.9 114.2 all-reduce.2
  334.1 111.4 all-reduce.4
